TPU v7x, 256 devices: a whole 4x4x8 slice. The times are simulated.
256 devices in a mesh: member: 16 (over y, x), region: 16 (over z, core).
Axes of the slice: x: 4, y: 4, z: 8, core: 2. Of those that a mesh axis runs over, the one named last changes fastest.
Arguments:
- states: float32 [512, 262144], P('member', 'region'), may hold values from -6 to 6
- obs_ens: float32 [512, 16384], P('member', 'region'), may hold values from -6 to 6
- innovation: float32 [512, 16384], P('member', 'region'), may hold values from -3 to 3
- lists: int32 [2048, 24], P('region'), may hold values from 0 to 127, as said below
- counts: int32 [2048], P('region'), may hold values from 1 to 24, as said below
- taper: float32 [2048, 24], P('region'), may hold values from 0.2 to 1
Outputs:
- analysis: float32 [512, 262144], P('member', 'region')
Inputs may be any that keep to these rules, and one draw needn't show every extreme that they name: `lists`: cell block c lies in region r = c // (8 * 16); its listed ids name observation blocks of regions r - 1, r or r + 1 (those that exist), region q owning blocks q*8 to (q+1)*8 - 1; ids may repeat, and a repeat counts again. Entries at positions counts[c] and beyond of lists and taper are not used; some cell block uses all 24.
All inputs are finite; a program needn't handle non-finite values.
Results may differ from a plain program's by a relative error of at most 0.0003.
Values sent between devices are 32-bit elements; how exact they have to be, the bound alone decides.
A program may use at most 128 MiB of HBM per device.

v0:
```python
import jax
import jax.numpy as jnp
from jax import lax
from jax.sharding import PartitionSpec as P

BLK = 128


def padded(block, sides, width):
    for axis, dim in sides:
        count = lax.axis_size(axis)
        forward = [(i, i + 1) for i in range(count - 1)]
        backward = [(target, source) for source, target in forward]
        low = lax.ppermute(
            lax.slice_in_dim(block, block.shape[dim] - width, None, axis=dim), axis, forward
        )
        high = lax.ppermute(lax.slice_in_dim(block, 0, width, axis=dim), axis, backward)
        block = jnp.concatenate([low, block, high], axis=dim)
    return block


def local(states, obs_ens, innovation, lists, counts, taper):
    members_local, cells_local = states.shape
    group = lax.axis_size("member")
    member_index = lax.axis_index("member")
    region_index = lax.axis_index("region")
    per_device = cells_local // (BLK * group)
    members = members_local * group
    highest = lax.Precision.HIGHEST
    positions = jnp.arange(per_device, dtype=jnp.int32)
    columns = lax.all_to_all(states, "member", split_axis=1, concat_axis=0, tiled=True)
    local_rows = member_index * per_device + positions
    anomalies = columns - jnp.mean(columns, axis=0, keepdims=True)
    stacked = jnp.stack((obs_ens, innovation))
    width = stacked.shape[2]
    full = lax.all_gather(stacked, "member", axis=1, tiled=True)
    centred = jnp.stack((full[0] - jnp.mean(full[0], axis=0, keepdims=True), full[1]))
    widened = padded(centred, (("region", 2),), width)
    obs_wide = widened[0]
    inn_wide = widened[1]
    first_block = (region_index - 1) * (width // BLK)

    def one_block(position, result):
        row_index = local_rows[position]
        start = position * BLK
        column = lax.dynamic_slice_in_dim(anomalies, start, BLK, 1)
        block_ids = lists[row_index]
        weights = taper[row_index]
        in_use = counts[row_index]

        def one_pair(entry, total):
            offset = (block_ids[entry] - first_block) * BLK
            obs_piece = lax.dynamic_slice_in_dim(obs_wide, offset, BLK, 1)
            inn_piece = lax.dynamic_slice_in_dim(inn_wide, offset, BLK, 1)
            cross = lax.dot_general(obs_piece, column, (((0,), (0,)), ((), ())), precision=highest)
            return total + jnp.dot(inn_piece, cross * weights[entry], precision=highest)

        total = lax.fori_loop(0, in_use, one_pair, jnp.zeros((members, BLK), jnp.float32))
        updated = lax.dynamic_slice_in_dim(columns, start, BLK, 1) + total / (members - 1.0)
        return lax.dynamic_update_slice_in_dim(result, updated, start, 1)

    analysed = lax.fori_loop(0, per_device, one_block, columns)
    return lax.all_to_all(analysed, "member", split_axis=0, concat_axis=1, tiled=True)


def solution(mesh):
    return jax.shard_map(
        local,
        mesh=mesh,
        in_specs=(
            P("member", "region"),
            P("member", "region"),
            P("member", "region"),
            P("region", None),
            P("region"),
            P("region", None),
        ),
        out_specs=P("member", "region"),
        check_vma=False,
    )
```

profile of v0, /device:TPU:104, one launch (start us, length us, event | category | flops | bytes accessed | tf_op | source)
XLA Modules:
  0.0 1332.5 jit_solution(8642899032880389342)
XLA Ops:
  8.2 59.9 %all-gather.2.cloned.1.call-done = f32[2,512,1024]{2,1,0:T(8,128)} async-done(((f32[2,32,1024]{2,1,0:T(8,128)}), f32[2,512,1024]{2,1,0:T(8,128)}) %all-gather.2.cloned.1.call-update) | async-done | bytes 4194320 | tf_op jit(solution)/shard_map/all_gather | solution.py:36
  69.9 2.8 slice_subtract_fusion
  72.8 2.4 pad_maximum_fusion.1
  78.1 3.6 collective-permute-start.1
  83.2 5.9 all-to-all-start
  89.3 33.2 %all-to-all-done = f32[32,16,1024]{2,0,1:T(8,128)S(1)} async-done(((f32[32,16,1024]{2,0,1:T(8,128)}), f32[32,16,1024]{2,0,1:T(8,128)S(1)}, u32[]{:S(2)}, u32[]{:S(2)}) %all-to-all-start) | async-done | bytes 2097184 | tf_op jit(solution)/shard_map/all_to_all | solution.py:31
  128.1 8.5 pad_maximum_fusion
  136.6 10.7 slice_bitcast_fusion
  147.3 230.3 %while.36 = (s32[]{:T(128)}, f32[512,1024]{1,0:T(8,128)}, f32[512,1024]{1,0:T(8,128)S(1)}, s32[8]{0:T(128)S(1)}, s32[128]{0:T(128)S(1)}, /*index=5*/s32[128,24]{...) while((s32[]{:T(128)}, f32[512,1024]{1,0:T(8,128)}, ...), condition=%wide.region_5.0_spmd, body=%wide.region_2.0_spmd.sunk | while | flops 201539584 | bytes 3016242 | solution.py:62
  151.2 18.8 %while.37 = (s32[]{:T(128)}, f32[512,128]{1,0:T(8,128)S(1)}, s32[]{:T(128)}, s32[24]{0:T(128)S(1)}, s32[]{:T(128)}, /*index=5*/f32[512,3072]{1,0:T(8,128)}, f32[...) while((s32[]{:T(128)}, f32[512,128]{1,0:T(8,128)S(1)}, ...), condition=%wide.region_4.0_spmd, body=%wide.region_3.0_spmd.sunk | while | flops 201408512 | bytes 1442561 | solution.py:58
  153.7 2.2 convolution_multiply_fusion.2
  159.8 2.2 convolution_multiply_fusion.2
  165.9 2.2 convolution_multiply_fusion.2
  174.6 18.8 %while.37 = (s32[]{:T(128)}, f32[512,128]{1,0:T(8,128)S(1)}, s32[]{:T(128)}, s32[24]{0:T(128)S(1)}, s32[]{:T(128)}, /*index=5*/f32[512,3072]{1,0:T(8,128)}, f32[...) while((s32[]{:T(128)}, f32[512,128]{1,0:T(8,128)S(1)}, ...), condition=%wide.region_4.0_spmd, body=%wide.region_3.0_spmd.sunk | while | flops 201408512 | bytes 1442561 | solution.py:58
  177.1 2.2 convolution_multiply_fusion.2
  183.2 2.2 convolution_multiply_fusion.2
  189.3 2.2 convolution_multiply_fusion.2
  198.1 31.0 %while.37 = (s32[]{:T(128)}, f32[512,128]{1,0:T(8,128)S(1)}, s32[]{:T(128)}, s32[24]{0:T(128)S(1)}, s32[]{:T(128)}, /*index=5*/f32[512,3072]{1,0:T(8,128)}, f32[...) while((s32[]{:T(128)}, f32[512,128]{1,0:T(8,128)S(1)}, ...), condition=%wide.region_4.0_spmd, body=%wide.region_3.0_spmd.sunk | while | flops 201408512 | bytes 1442561 | solution.py:58
  200.6 2.2 convolution_multiply_fusion.2
  206.7 2.2 convolution_multiply_fusion.2
  212.8 2.2 convolution_multiply_fusion.2
  218.9 2.2 convolution_multiply_fusion.2
  225.0 2.2 convolution_multiply_fusion.2
  233.7 24.9 %while.37 = (s32[]{:T(128)}, f32[512,128]{1,0:T(8,128)S(1)}, s32[]{:T(128)}, s32[24]{0:T(128)S(1)}, s32[]{:T(128)}, /*index=5*/f32[512,3072]{1,0:T(8,128)}, f32[...) while((s32[]{:T(128)}, f32[512,128]{1,0:T(8,128)S(1)}, ...), condition=%wide.region_4.0_spmd, body=%wide.region_3.0_spmd.sunk | while | flops 201408512 | bytes 1442561 | solution.py:58
  236.3 2.2 convolution_multiply_fusion.2
  242.3 2.2 convolution_multiply_fusion.2
  248.4 2.2 convolution_multiply_fusion.2
  254.5 2.2 convolution_multiply_fusion.2
  263.3 49.2 %while.37 = (s32[]{:T(128)}, f32[512,128]{1,0:T(8,128)S(1)}, s32[]{:T(128)}, s32[24]{0:T(128)S(1)}, s32[]{:T(128)}, /*index=5*/f32[512,3072]{1,0:T(8,128)}, f32[...) while((s32[]{:T(128)}, f32[512,128]{1,0:T(8,128)S(1)}, ...), condition=%wide.region_4.0_spmd, body=%wide.region_3.0_spmd.sunk | while | flops 201408512 | bytes 1442561 | solution.py:58
  265.8 2.2 convolution_multiply_fusion.2
  271.9 2.2 convolution_multiply_fusion.2
  278.0 2.2 convolution_multiply_fusion.2
  284.1 2.2 convolution_multiply_fusion.2
  296.2 2.2 convolution_multiply_fusion.2
  302.3 2.2 convolution_multiply_fusion.2
  308.4 2.2 convolution_multiply_fusion.2
  317.2 18.8 %while.37 = (s32[]{:T(128)}, f32[512,128]{1,0:T(8,128)S(1)}, s32[]{:T(128)}, s32[24]{0:T(128)S(1)}, s32[]{:T(128)}, /*index=5*/f32[512,3072]{1,0:T(8,128)}, f32[...) while((s32[]{:T(128)}, f32[512,128]{1,0:T(8,128)S(1)}, ...), condition=%wide.region_4.0_spmd, body=%wide.region_3.0_spmd.sunk | while | flops 201408512 | bytes 1442561 | solution.py:58
  319.7 2.2 convolution_multiply_fusion.2
  325.8 2.2 convolution_multiply_fusion.2
  331.9 2.2 convolution_multiply_fusion.2
  340.6 24.9 %while.37 = (s32[]{:T(128)}, f32[512,128]{1,0:T(8,128)S(1)}, s32[]{:T(128)}, s32[24]{0:T(128)S(1)}, s32[]{:T(128)}, /*index=5*/f32[512,3072]{1,0:T(8,128)}, f32[...) while((s32[]{:T(128)}, f32[512,128]{1,0:T(8,128)S(1)}, ...), condition=%wide.region_4.0_spmd, body=%wide.region_3.0_spmd.sunk | while | flops 201408512 | bytes 1442561 | solution.py:58
  343.2 2.2 convolution_multiply_fusion.2
  349.2 2.2 convolution_multiply_fusion.2
  355.3 2.2 convolution_multiply_fusion.2
  361.4 2.2 convolution_multiply_fusion.2
  370.2 6.6 while.37
  372.7 2.2 convolution_multiply_fusion.2
  377.6 946.5 %all_to_all.38 = f32[16,32,1024]{2,1,0:T(8,128)S(1)} all-to-all(f32[16,32,1024]{2,1,0:T(8,128)} %bitcast.47), channel_id=1, replica_groups=mesh['member'=16,'region'=16] {'member'}, dimensions={0} | all-to-all | bytes 4194304 | tf_op jit(solution)/shard_map/all_to_all | solution.py:63
  (183 shorter events, 124.5 us)
Async XLA Ops:
  6.5 61.6 %all-gather.2.cloned.1.call-start = ((), (), s32[]{:S(2)}) async-start(), calls=%async_computation.2 | async-start | bytes 4456448 | tf_op jit(solution)/shard_map/all_gather | solution.py:36
  72.7 2.7 copy-start
  72.8 3.4 copy-start.2
  72.8 9.0 copy-start.4
  76.2 50.1 %collective-permute-start = (f32[2,512,1024]{2,1,0:T(8,128)}, f32[2,512,1024]{2,1,0:T(8,128)}, u32[]{:S(2)}, u32[]{:S(2)}) collective-permute-start(f32[2,512,1024]{2,1,0:T(8,128)} %pad_maximum_fusion.1), channel_id=1, source_target_pairs={{0,1},{1,2},{2,3},{3,4},{4,5},{5,6},{6,7},{7,8},{8,9},{9,10},{10,1... | collective-permute-start | bytes 12582920 | tf_op jit(solution)/shard_map/ppermute | solution.py:14
  78.1 50.0 %collective-permute-start.1 = (f32[2,512,1024]{2,1,0:T(8,128)}, f32[2,512,1024]{2,1,0:T(8,128)}, u32[]{:S(2)}, u32[]{:S(2)}) collective-permute-start(f32[2,512,1024]{2,1,0:T(8,128)} %pad_maximum_fusion.1), channel_id=1, source_target_pairs={{1,0},{2,1},{3,2},{4,3},{5,4},{6,5},{7,6},{8,7},{9,8},{10,9},{11,1... | collective-permute-start | bytes 12582920 | tf_op jit(solution)/shard_map/ppermute | solution.py:17
  83.2 5.9 copy-start.5
  83.2 6.0 copy-start.6
  83.2 39.3 %all-to-all-start = ((f32[32,16,1024]{2,0,1:T(8,128)}), f32[32,16,1024]{2,0,1:T(8,128)S(1)}, u32[]{:S(2)}, u32[]{:S(2)}) async-start(f32[32,16,1024]{2,0,1:T(8,128)} %bitcast.46), calls=%async_computation | async-start | bytes 4194304 | tf_op jit(solution)/shard_map/all_to_all | solution.py:31
  124.0 4.1 copy-start.1
  124.0 4.1 copy-start.3
  136.6 10.7 copy-start.7
Sparse Core Ops, SparseCore 0:
  9.8 58.3 all-gather.1
where the time goes:
time: 1360 us; the launch traced here: 1330 us
  blocking collectives  947 us (70%)
  matrix products  110 us (8%)
  waiting for transfers between devices  95.5 us (7%)
  local copies, waits for them, and re-layouts  74 us (5%)
  loops' own time  56.2 us (4%)
  other arithmetic  25.1 us (2%)
    all_to_all x1, blocking collectives, local(): lax.all_to_all(analysed, 'member', split_axis=0, concat_axis=1, tiled=True)  947 us
    dot_general x31, matrix products, one_pair(): lax.dot_general(obs_piece, column, (((0,), (0,)), ((), ())), precision=hi...  67 us
    all_gather x1, waiting for transfers between devices, local(): full = lax.all_gather(stacked, 'member', axis=1, tiled=True)  59.9 us
    dot_general x31, matrix products, one_pair(): return total + jnp.dot(inn_piece, cross * weights[entry], precision=highest)  43.4 us
    another operation x8, loops' own time, one_block(): lax.fori_loop(0, in_use, one_pair, jnp.zeros((members, BLK), jnp.float32))  42.4 us
    all_to_all x1, waiting for transfers between devices, local(): lax.all_to_all(states, 'member', split_axis=1, concat_axis=0, tiled=True)  33.2 us
  transfers between devices with their start and end apart: 4, of which 4 were waited for; matrix products, arithmetic and copies ran while one was open for 0% of the time, Pallas kernels for 0%

commit v1 on v0

v1 whole, which is shorter than its diff:
```python
import jax
import jax.numpy as jnp
from jax import lax
from jax.experimental import pallas as pl
from jax.experimental.pallas import tpu as pltpu
from jax.sharding import PartitionSpec as P

MESH = pl.DeviceIdType.MESH
BLK = 128
NX = 4
NY = 4
GROUP = NX * NY
ROWS = 32
MEMBERS = 512
CELLS = 1024
CB = CELLS // BLK
OBS = 1024
OB = OBS // BLK
HALF = OBS // 2
L = 24
SENDS = 4
WIDE = CELLS // SENDS


def split(value):
    high = value.astype(jnp.bfloat16)
    return high, (value - high.astype(jnp.float32)).astype(jnp.bfloat16)


def kernel(
    states, obs, inn, lists, counts, taper, out,
    wide, cols, cells_hl, g, w, table, result,
    local_sem, g_send, g_recv, f_send, f_recv, a_send, a_recv, o_send, o_recv,
):
    member = lax.axis_index("member")
    region = lax.axis_index("region")
    regions = lax.axis_size("region")
    y, x = member // NX, member % NX
    core = region % 2
    above = lax.rem(region + 1, regions)
    below = lax.rem(region + regions - 1, regions)

    def at(yy, xx):
        return (lax.rem(yy, NY) * NX + lax.rem(xx, NX), region)

    own_obs = pltpu.make_async_copy(obs, wide.at[1, 0, y, x], local_sem.at[0])
    own_inn = pltpu.make_async_copy(inn, wide.at[1, 1, y, x], local_sem.at[1])
    own_cols = pltpu.make_async_copy(
        states.at[:, pl.ds(pl.multiple_of(member * CELLS, CELLS), CELLS)], cols.at[member], local_sem.at[2]
    )
    own_obs.start()
    own_inn.start()
    own_cols.start()

    barrier = pltpu.get_barrier_semaphore()
    for k in range(1, GROUP):
        pl.semaphore_signal(barrier, inc=1, device_id=at(y + k // NX, x + k % NX), device_id_type=MESH)
    for other in (above, below):
        pl.semaphore_signal(barrier, inc=1, device_id=(member, other), device_id_type=MESH)
    pl.semaphore_wait(barrier, GROUP + 1)

    first_half, second_half = pl.ds(0, HALF), pl.ds(HALF, HALF)

    def remote(source, target, send, recv, device):
        return pltpu.make_async_remote_copy(
            src_ref=source, dst_ref=target, send_sem=send, recv_sem=recv, device_id=device, device_id_type=MESH
        )

    def gather(phase, half, d):
        if phase == 0:
            piece = wide.at[1, :, y, x, :, first_half if half == 0 else second_half]
        elif half == 0:
            piece = wide.at[1, :, y, :, :, first_half]
        else:
            piece = wide.at[1, :, :, x, :, second_half]
        along_x = (phase == 0) == (half == 0)
        n = phase * 6 + half * 3 + d - 1
        return remote(piece, piece, g_send.at[n], g_recv.at[n], at(y, x + d) if along_x else at(y + d, x))

    def piece_of(slot, piece):
        if piece == 0:
            return wide.at[slot, :, y, x]
        phase, half, d = (piece - 1) // 6, (piece - 1) // 3 % 2, (piece - 1) % 3 + 1
        cut = first_half if half == 0 else second_half
        yy, xx = lax.rem(y + NY - d, NY), lax.rem(x + NX - d, NX)
        if phase == 0:
            return wide.at[slot, :, y, xx, :, cut] if half == 0 else wide.at[slot, :, yy, x, :, cut]
        return wide.at[slot, :, yy, :, :, cut] if half == 0 else wide.at[slot, :, :, xx, :, cut]

    def pass_on(piece, slot, n):
        return remote(
            piece_of(1, piece), piece_of(slot, piece), f_send.at[n, piece], f_recv.at[n, piece],
            (member, above if n == 0 else below),
        )

    def cells_in(k):
        yy, xx = lax.rem(y + k // NX, NY), lax.rem(x + k % NX, NX)
        target = yy * NX + xx
        return remote(
            states.at[:, pl.ds(pl.multiple_of(target * CELLS, CELLS), CELLS)], cols.at[member],
            a_send.at[k - 1], a_recv.at[k - 1], (target, region),
        )

    def cells_out(part, k):
        yy, xx = lax.rem(y + k // NX, NY), lax.rem(x + k % NX, NX)
        target = yy * NX + xx
        place = pl.multiple_of(member * CELLS + part * WIDE, WIDE)
        return remote(
            result.at[target, :, pl.ds(part * WIDE, WIDE)], out.at[:, pl.ds(place, WIDE)],
            o_send.at[part, k - 1], o_recv.at[part, k - 1], (target, region),
        )

    def both(piece):
        pass_on(piece, 0, 0).start()
        pass_on(piece, 2, 1).start()

    own_obs.wait()
    own_inn.wait()
    for d in (1, 3, 2):
        for half in (0, 1):
            gather(0, half, d).start()
    both(0)
    for d in (1, 3, 2):
        for half in (0, 1):
            gather(0, half, d).wait_recv()
            both(1 + half * 3 + d - 1)
    for d in (1, 3, 2):
        for half in (0, 1):
            gather(1, half, d).start()
    for k in range(1, GROUP):
        cells_in(k).start()

    start = pl.multiple_of(member * CB, CB)
    ids = lists[pl.ds(start, CB), :] - (region - 1) * OB
    rows = lax.broadcasted_iota(jnp.int32, (CB, L), 0)
    used = jnp.zeros((CB, L), jnp.int32)
    for i in range(CB):
        used = jnp.where(rows == i, counts[start + i], used)
    in_use = lax.broadcasted_iota(jnp.int32, (CB, L), 1) < used
    weights = jnp.where(in_use, taper[pl.ds(start, CB), :], 0.0) * (1.0 / (MEMBERS - 1.0))
    for b in range(3 * OB):
        total = jnp.sum(jnp.where(ids == b, weights, 0.0), axis=1, keepdims=True)
        table[b] = jnp.broadcast_to(total, (CB, BLK))

    for d in (1, 3, 2):
        for half in (0, 1):
            gather(1, half, d).wait_recv()
            both(7 + half * 3 + d - 1)

    def window(slot, first):
        def block(b, carry):
            at_b = pl.ds(pl.multiple_of(b * BLK, BLK), BLK)
            o = wide[slot, 0, :, :, :, at_b].reshape(MEMBERS, BLK)
            o_hi, o_lo = split(o - jnp.mean(o, axis=0, keepdims=True))
            i_hi, i_lo = split(wide[slot, 1, :, :, :, at_b].reshape(MEMBERS, BLK))
            g[b] = lax.dot_general(
                jnp.concatenate([i_hi, i_lo, i_hi], axis=1), jnp.concatenate([o_hi, o_hi, o_lo], axis=1),
                (((1,), (1,)), ((), ())), preferred_element_type=jnp.float32,
            )
            return carry

        lax.fori_loop(0, OB, block, 0)

        def strip(i, carry):
            at_i = pl.ds(pl.multiple_of(i * 8, 8), 8)
            lanes = [pl.ds(k * BLK, BLK) for k in range(MEMBERS // BLK)]
            parts = [[g[b, at_i, lane] for lane in lanes] for b in range(OB)]
            for c in range(CB):
                sums = [None if first else w[c, at_i, lane] for lane in lanes]
                for b in range(OB):
                    weight = jnp.broadcast_to(table[slot * OB + b, pl.ds(c, 1), :], (8, BLK))
                    sums = [
                        part * weight if old is None else old + part * weight for old, part in zip(sums, parts[b])
                    ]
                for lane, new in zip(lanes, sums):
                    w[c, at_i, lane] = new
            return carry

        lax.fori_loop(0, MEMBERS // 8, strip, 0)

    window(1, True)
    near, far = 2 - 2 * core, 2 * core
    for piece in range(13):
        pass_on(piece, 0, 0).wait_send()
        pass_on(piece, 2, 1).wait_send()

    def arrived(slot):
        for piece in range(13):
            target = piece_of(slot, piece)
            remote(
                target, target, f_send.at[slot // 2, piece], f_recv.at[slot // 2, piece], (member, above)
            ).wait_recv()

    arrived(near)
    window(near, False)

    own_cols.wait()
    for k in range(1, GROUP):
        cells_in(k).wait_recv()

    def centre(c, carry):
        at_c = pl.ds(pl.multiple_of(c * BLK, BLK), BLK)
        a = cols[:, :, at_c].reshape(MEMBERS, BLK)
        hi, lo = split(a - jnp.mean(a, axis=0, keepdims=True))
        cells_hl[c] = jnp.concatenate([hi, lo], axis=1)
        return carry

    lax.fori_loop(0, CB, centre, 0)

    arrived(far)
    window(far, False)

    own_out = []
    for part in range(SENDS):
        def finish(c, carry):
            at_c = pl.ds(pl.multiple_of(c * BLK, BLK), BLK)
            hi, lo = split(w[c])
            a = cells_hl[c]
            both_ = jnp.dot(hi, a, preferred_element_type=jnp.float32)
            low = jnp.dot(lo, a[:, :BLK], preferred_element_type=jnp.float32)
            inc = both_[:, :BLK] + (both_[:, BLK:] + low)
            result[:, :, at_c] = cols[:, :, at_c] + inc.reshape(GROUP, ROWS, BLK)
            return carry

        lax.fori_loop(part * (CB // SENDS), (part + 1) * (CB // SENDS), finish, 0)
        for k in range(1, GROUP):
            cells_out(part, k).start()
    place = pl.multiple_of(member * CELLS, CELLS)
    keep = pltpu.make_async_copy(result.at[member], out.at[:, pl.ds(place, CELLS)], local_sem.at[3])
    keep.start()

    for phase in (0, 1):
        for half in (0, 1):
            for d in (1, 2, 3):
                gather(phase, half, d).wait_send()
    for k in range(1, GROUP):
        cells_in(k).wait_send()
    for part in range(SENDS):
        for k in range(1, GROUP):
            cells_out(part, k).wait()
    keep.wait()


def local(states, obs_ens, innovation, lists, counts, taper):
    hbm = pl.BlockSpec(memory_space=pl.ANY)
    vmem = pl.BlockSpec(memory_space=pltpu.VMEM)
    smem = pl.BlockSpec(memory_space=pltpu.SMEM)
    dma = pltpu.SemaphoreType.DMA
    return pl.pallas_call(
        kernel,
        out_shape=jax.ShapeDtypeStruct(states.shape, jnp.float32),
        in_specs=[hbm, hbm, hbm, vmem, smem, vmem],
        out_specs=hbm,
        scratch_shapes=[
            pltpu.VMEM((3, 2, NY, NX, ROWS, OBS), jnp.float32),
            pltpu.VMEM((GROUP, ROWS, CELLS), jnp.float32),
            pltpu.VMEM((CB, MEMBERS, 2 * BLK), jnp.bfloat16),
            pltpu.VMEM((OB, MEMBERS, MEMBERS), jnp.float32),
            pltpu.VMEM((CB, MEMBERS, MEMBERS), jnp.float32),
            pltpu.VMEM((3 * OB, CB, BLK), jnp.float32),
            pltpu.VMEM((GROUP, ROWS, CELLS), jnp.float32),
            dma((4,)),
            dma((12,)),
            dma((12,)),
            dma((2, 13)),
            dma((2, 13)),
            dma((GROUP - 1,)),
            dma((GROUP - 1,)),
            dma((SENDS, GROUP - 1)),
            dma((SENDS, GROUP - 1)),
        ],
        compiler_params=pltpu.CompilerParams(
            collective_id=0, has_side_effects=True, vmem_limit_bytes=56 * 2**20
        ),
        name="analysis",
    )(states, obs_ens, innovation, lists, counts, taper)


def solution(mesh):
    return jax.shard_map(
        local,
        mesh=mesh,
        in_specs=(
            P("member", "region"),
            P("member", "region"),
            P("member", "region"),
            P("region", None),
            P("region"),
            P("region", None),
        ),
        out_specs=P("member", "region"),
        check_vma=False,
    )
```

time: 1360 us -> 125 us (0.09); the launches traced: 1330 us -> 124 us
  blocking collectives: 947 us -> 0 us
  Pallas kernels: 0 us -> 118 us
  matrix products: 110 us -> 0 us
  waiting for transfers between devices: 95.5 us -> 0 us
  local copies, waits for them, and re-layouts: 74 us -> 5.9 us
  loops' own time: 56.2 us -> 0 us
  other arithmetic: 25.1 us -> 0 us
    all_to_all x1 -> x0, blocking collectives: 947 us -> none  [local(): lax.all_to_all(analysed, 'member', split_axis=0, concat_axis=1, tiled=True)]
    pallas_call x0 -> x1, Pallas kernels: none -> 118 us  [local(): pl.pallas_call(kernel, out_shape=jax.ShapeDtypeStruct(states.shape, jnp.f...]
    dot_general x62 -> x0, matrix products: 110 us -> none  [the longest x31 67 us: one_pair(): lax.dot_general(obs_piece, column, (((0,), (0,)), ((), ())), precision=hi...]
    all_gather x1 -> x0, waiting for transfers between devices: 59.9 us -> none  [local(): full = lax.all_gather(stacked, 'member', axis=1, tiled=True)]
    dynamic_slice x86 -> x0, local copies, waits for them, and re-layouts: 57.4 us -> none  [the longest x31 20.1 us: one_pair(): return total + jnp.dot(inn_piece, cross * weights[entry], precision=highest)]
    another operation x9 -> x0, loops' own time: 56.2 us -> none  [the longest x8 42.4 us: one_block(): lax.fori_loop(0, in_use, one_pair, jnp.zeros((members, BLK), jnp.float32))]
    all_to_all x1 -> x0, waiting for transfers between devices: 33.2 us -> none  [local(): lax.all_to_all(states, 'member', split_axis=1, concat_axis=0, tiled=True)]
  transfers between devices with their start and end apart: 4 -> 0, of which waited for: 4 -> 0; matrix products, arithmetic and copies ran while one was open for 0% -> 0% of each run, Pallas kernels for 0% -> 0%
where the time goes in v1:
time: 125 us; the launch traced here: 124 us
  Pallas kernels  118 us (94%)
  local copies, waits for them, and re-layouts  5.9 us (5%)
    pallas_call x1, Pallas kernels, local(): pl.pallas_call(kernel, out_shape=jax.ShapeDtypeStruct(states.shape, jnp.f...  118 us
    unnamed x3, local copies, waits for them, and re-layouts  5.9 us

profile of v1, /device:TPU:104, one launch (start us, length us, event | category | flops | bytes accessed | tf_op | source)
XLA Modules:
  0.0 123.9 jit_solution(4559117567335554797)
XLA Ops:
  0.0 1.4 %copy.7.lists = s32[128,24]{1,0:T(8,128)} copy(s32[128,24]{0,1:T(8,128)} %param.9) | data formatting | bytes 24576 | tf_op args[3]
  1.4 1.4 %copy.8.taper = f32[128,24]{1,0:T(8,128)} copy(f32[128,24]{0,1:T(8,128)} %param.11) | data formatting | bytes 24576 | tf_op args[5]
  2.9 118.0 %analysis.1 = f32[32,16384]{1,0:T(8,128)} custom-call(f32[32,16384]{1,0:T(8,128)} %states.1, f32[32,1024]{1,0:T(8,128)} %obs.1, f32[32,1024]{1,0:T(8,128)} %inn.1, s32[128,24]{1,0:T(8,128)} %copy.7.lists, s32[128]{0:T(128)} %counts.1, f32[128,24]{1,0:T(8,128)} %copy.8.taper), custom_call_target="tpu_custom_call" | custom-call | tf_op jit(solution)/shard_map/analysis/pallas_call | solution.py:249
  120.8 3.0 %copy.10 = f32[32,16384]{1,0:T(8,128)} copy(f32[32,16384]{1,0:T(8,128)} %analysis.1) | data formatting | bytes 4194304

commit v2 on v1

v2 whole, which is shorter than its diff:
```python
import jax
import jax.numpy as jnp
from jax import lax
from jax.experimental import pallas as pl
from jax.experimental.pallas import tpu as pltpu
from jax.sharding import PartitionSpec as P

MESH = pl.DeviceIdType.MESH
BLK = 128
NX = 4
NY = 4
GROUP = NX * NY
ROWS = 32
MEMBERS = 512
CELLS = 1024
CB = CELLS // BLK
OBS = 1024
OB = OBS // BLK
QUART = OBS // 4
QB = OB // 2
L = 24
SENDS = 4
ORDER = (1, 4, 3, 12, 5, 15, 7, 13, 2, 8, 6, 9, 14, 11, 10)
WIDE = CELLS // SENDS


def split(value):
    high = value.astype(jnp.bfloat16)
    return high, (value - high.astype(jnp.float32)).astype(jnp.bfloat16)


def kernel(
    states, obs, inn, lists, counts, taper, out,
    wide, cols, cells_hl, g, w, table, result,
    local_sem, g_send, g_recv, f_send, f_recv, a_send, a_recv, o_send, o_recv,
):
    member = lax.axis_index("member")
    region = lax.axis_index("region")
    regions = lax.axis_size("region")
    y, x = member // NX, member % NX
    core = region % 2
    above = lax.rem(region + 1, regions)
    below = lax.rem(region + regions - 1, regions)

    def at(yy, xx):
        return (lax.rem(yy, NY) * NX + lax.rem(xx, NX), region)

    own_obs = pltpu.make_async_copy(obs, wide.at[1, 0, y, x], local_sem.at[0])
    own_inn = pltpu.make_async_copy(inn, wide.at[1, 1, y, x], local_sem.at[1])
    own_cols = pltpu.make_async_copy(
        states.at[:, pl.ds(pl.multiple_of(member * CELLS, CELLS), CELLS)], cols.at[member], local_sem.at[2]
    )
    own_obs.start()
    own_inn.start()
    own_cols.start()

    barrier = pltpu.get_barrier_semaphore()
    for k in range(1, GROUP):
        pl.semaphore_signal(barrier, inc=1, device_id=at(y + k // NX, x + k % NX), device_id_type=MESH)
    for other in (above, below):
        pl.semaphore_signal(barrier, inc=1, device_id=(member, other), device_id_type=MESH)
    pl.semaphore_wait(barrier, GROUP + 1)

    def cut(q):
        return pl.ds(q * QUART, QUART)

    def remote(source, target, send, recv, device):
        return pltpu.make_async_remote_copy(
            src_ref=source, dst_ref=target, send_sem=send, recv_sem=recv, device_id=device, device_id_type=MESH
        )

    def line(slot, q, d):
        if q % 2 == 0:
            return wide.at[slot, :, y, lax.rem(x + d, NX), :, cut(q)]
        return wide.at[slot, :, lax.rem(y + d, NY), x, :, cut(q)]

    def plane(slot, q, d, kind=slice(None)):
        if q % 2 == 0:
            return wide.at[slot, kind, lax.rem(y + d, NY), :, :, cut(q)]
        return wide.at[slot, kind, :, lax.rem(x + d, NX), :, cut(q)]

    def along(q, hop, d):
        return at(y, x + d) if (q + hop) % 2 == 0 else at(y + d, x)

    def first(q, d):
        piece = line(1, q, 0)
        return remote(piece, piece, g_send.at[q, d - 1], g_recv.at[q, d - 1], along(q, 0, d))

    def second(q, d):
        piece = plane(1, q, 0)
        return remote(piece, piece, g_send.at[q, 2 + d], g_recv.at[q, 2 + d], along(q, 1, d))

    def relay(q, d):
        piece = plane(1, q, 4 - d, d // 2)
        return remote(piece, piece, g_send.at[q, 6 + d // 2], g_recv.at[q, 6 + d // 2], along(q, 1, d))

    def piece_of(slot, piece):
        if piece == 0:
            return wide.at[slot, :, y, x]
        if piece < 13:
            return line(slot, (piece - 1) // 3, (piece - 1) % 3 + 1)
        return plane(slot, (piece - 13) // 3, (piece - 13) % 3 + 1)

    def pass_on(piece, slot, n):
        return remote(
            piece_of(1, piece), piece_of(slot, piece), f_send.at[n, piece], f_recv.at[n, piece],
            (member, above if n == 0 else below),
        )

    def cells_in(k):
        yy, xx = lax.rem(y + k // NX, NY), lax.rem(x + k % NX, NX)
        target = yy * NX + xx
        return remote(
            states.at[:, pl.ds(pl.multiple_of(target * CELLS, CELLS), CELLS)], cols.at[member],
            a_send.at[k - 1], a_recv.at[k - 1], (target, region),
        )

    def cells_out(part, k):
        yy, xx = lax.rem(y + k // NX, NY), lax.rem(x + k % NX, NX)
        target = yy * NX + xx
        place = pl.multiple_of(member * CELLS + part * WIDE, WIDE)
        return remote(
            result.at[target, :, pl.ds(part * WIDE, WIDE)], out.at[:, pl.ds(place, WIDE)],
            o_send.at[part, k - 1], o_recv.at[part, k - 1], (target, region),
        )

    def both(piece):
        pass_on(piece, 0, 0).start()
        pass_on(piece, 2, 1).start()

    def lines(pair):
        for d in (1, 3, 2):
            for q in pair:
                first(q, d).wait_recv()
                both(3 * q + 4 - d)
        for d in (1, 3):
            for q in pair:
                second(q, d).start()

    def planes_near(pair, onward=None):
        for d in (1, 3):
            for q in pair:
                second(q, d).wait_recv()
                relay(q, d).start()
                if onward is None or q in onward:
                    both(13 + 3 * q + 3 - d)

    def planes_far(pair, last=()):
        for q in pair:
            for d in (1, 3):
                relay(q, d).wait_recv()
            both(13 + 3 * q + 1)
            if q in last[1:]:
                both(13 + 3 * q)
                both(13 + 3 * q + 2)

    own_obs.wait()
    own_inn.wait()
    for pair in ((0, 1), (2, 3)):
        for d in (1, 3, 2):
            for q in pair:
                first(q, d).start()
    both(0)
    lines((0, 1))
    lines((2, 3))

    start = member * CB
    ids = lists[...] - (region - 1) * OB
    used = lax.broadcasted_iota(jnp.int32, (L, BLK), 0) < counts[...]
    weights = jnp.where(used, taper[...], 0.0) * (1.0 / (MEMBERS - 1.0))
    lane_of = lax.broadcasted_iota(jnp.int32, (CB, BLK), 1)
    mine = (lane_of == start + lax.broadcasted_iota(jnp.int32, (CB, BLK), 0)).astype(jnp.float32)
    for b in range(3 * OB):
        total = jnp.sum(jnp.where(ids == b, weights, 0.0), axis=0, keepdims=True)
        table[b] = jnp.broadcast_to(jnp.sum(mine * total, axis=1, keepdims=True), (CB, BLK))

    def products(runs):
        base = 0
        for slot, begin, many in runs:
            def block(b, carry, slot=slot, begin=begin, base=base):
                at_b = pl.ds(pl.multiple_of((begin + b) * BLK, BLK), BLK)
                o = wide[slot, 0, :, :, :, at_b].reshape(MEMBERS, BLK)
                o_hi, o_lo = split(o - jnp.mean(o, axis=0, keepdims=True))
                i_hi, i_lo = split(wide[slot, 1, :, :, :, at_b].reshape(MEMBERS, BLK))
                g[base + b] = lax.dot_general(
                    jnp.concatenate([i_hi, i_lo, i_hi], axis=1), jnp.concatenate([o_hi, o_hi, o_lo], axis=1),
                    (((1,), (1,)), ((), ())), preferred_element_type=jnp.float32,
                )
                return carry

            lax.fori_loop(0, many, block, 0, unroll=True)
            base += many

    def add(runs, new=False):
        rows = [slot * OB + begin + b for slot, begin, many in runs for b in range(many)]

        def strip(i, carry):
            at_i = pl.ds(pl.multiple_of(i * 8, 8), 8)
            lanes = [pl.ds(k * BLK, BLK) for k in range(MEMBERS // BLK)]
            parts = [[g[b, at_i, lane] for lane in lanes] for b in range(len(rows))]
            for c in range(CB):
                sums = [None if new else w[c, at_i, lane] for lane in lanes]
                for row, part in zip(rows, parts):
                    weight = jnp.broadcast_to(table[row, pl.ds(c, 1), :], (8, BLK))
                    sums = [p * weight if old is None else old + p * weight for old, p in zip(sums, part)]
                for lane, total in zip(lanes, sums):
                    w[c, at_i, lane] = total
            return carry

        lax.fori_loop(0, MEMBERS // 8, strip, 0, unroll=2)

    def window(*runs):
        products(runs)
        add(runs)

    near, far = 2 - 2 * core, 2 * core

    def arrived(slot, pieces):
        for piece in pieces:
            target = piece_of(slot, piece)
            remote(
                target, target, f_send.at[slot // 2, piece], f_recv.at[slot // 2, piece], (member, above)
            ).wait_recv()

    early = (*range(7), *range(13, 19))
    planes_near((0, 1))
    planes_far((0, 1))
    products([(1, 0, 4)])
    planes_near((2, 3), (2,))
    add([(1, 0, 4)], True)
    planes_far((2, 3), (2, 3))
    for k in ORDER:
        cells_in(k).start()
    arrived(near, early)
    window((near, 0, 4))
    arrived(near, (*range(7, 13), *range(19, 25)))
    window((1, 4, 4), (near, 4, 4))
    arrived(far, early)
    window((far, 0, 4))

    own_cols.wait()
    for k in range(1, GROUP):
        cells_in(k).wait_recv()

    def centre(c, carry):
        at_c = pl.ds(pl.multiple_of(c * BLK, BLK), BLK)
        a = cols[:, :, at_c].reshape(MEMBERS, BLK)
        hi, lo = split(a - jnp.mean(a, axis=0, keepdims=True))
        cells_hl[c] = jnp.concatenate([hi, lo], axis=1)
        return carry

    lax.fori_loop(0, CB, centre, 0)

    arrived(far, (*range(7, 10), *range(19, 22)))
    window((far, 4, 2))
    arrived(far, (*range(10, 13), *range(22, 25)))
    window((far, 6, 2))

    for part in range(SENDS):
        def finish(c, carry):
            at_c = pl.ds(pl.multiple_of(c * BLK, BLK), BLK)
            hi, lo = split(w[c])
            a = cells_hl[c]
            both_ = jnp.dot(hi, a, preferred_element_type=jnp.float32)
            low = jnp.dot(lo, a[:, :BLK], preferred_element_type=jnp.float32)
            inc = both_[:, :BLK] + (both_[:, BLK:] + low)
            result[:, :, at_c] = cols[:, :, at_c] + inc.reshape(GROUP, ROWS, BLK)
            return carry

        lax.fori_loop(part * (CB // SENDS), (part + 1) * (CB // SENDS), finish, 0)
        for k in ORDER:
            cells_out(part, k).start()
    place = pl.multiple_of(member * CELLS, CELLS)
    keep = pltpu.make_async_copy(result.at[member], out.at[:, pl.ds(place, CELLS)], local_sem.at[3])
    keep.start()

    for q in range(4):
        for d in (1, 2, 3):
            first(q, d).wait_send()
        for d in (1, 3):
            second(q, d).wait_send()
            relay(q, d).wait_send()
    for piece in range(25):
        pass_on(piece, 0, 0).wait_send()
        pass_on(piece, 2, 1).wait_send()
    for k in range(1, GROUP):
        cells_in(k).wait_send()
    for part in range(SENDS):
        for k in range(1, GROUP):
            cells_out(part, k).wait()
    keep.wait()


def local(states, obs_ens, innovation, lists, counts, taper):
    hbm = pl.BlockSpec(memory_space=pl.ANY)
    vmem = pl.BlockSpec(memory_space=pltpu.VMEM)
    dma = pltpu.SemaphoreType.DMA
    return pl.pallas_call(
        kernel,
        out_shape=jax.ShapeDtypeStruct(states.shape, jnp.float32),
        in_specs=[hbm, hbm, hbm, vmem, vmem, vmem],
        out_specs=hbm,
        scratch_shapes=[
            pltpu.VMEM((3, 2, NY, NX, ROWS, OBS), jnp.float32),
            pltpu.VMEM((GROUP, ROWS, CELLS), jnp.float32),
            pltpu.VMEM((CB, MEMBERS, 2 * BLK), jnp.bfloat16),
            pltpu.VMEM((OB, MEMBERS, MEMBERS), jnp.float32),
            pltpu.VMEM((CB, MEMBERS, MEMBERS), jnp.float32),
            pltpu.VMEM((3 * OB, CB, BLK), jnp.float32),
            pltpu.VMEM((GROUP, ROWS, CELLS), jnp.float32),
            dma((4,)),
            dma((4, 8)),
            dma((4, 8)),
            dma((2, 25)),
            dma((2, 25)),
            dma((GROUP - 1,)),
            dma((GROUP - 1,)),
            dma((SENDS, GROUP - 1)),
            dma((SENDS, GROUP - 1)),
        ],
        compiler_params=pltpu.CompilerParams(
            collective_id=0, has_side_effects=True, vmem_limit_bytes=56 * 2**20
        ),
        name="analysis",
    )(states, obs_ens, innovation, lists.T, counts.reshape(1, -1), taper.T)


def solution(mesh):
    return jax.shard_map(
        local,
        mesh=mesh,
        in_specs=(
            P("member", "region"),
            P("member", "region"),
            P("member", "region"),
            P("region", None),
            P("region"),
            P("region", None),
        ),
        out_specs=P("member", "region"),
        check_vma=False,
    )
```

time: 125 us -> 97.8 us (0.78)
  Pallas kernels: 118 us -> 94.6 us
  local copies, waits for them, and re-layouts: 5.9 us -> 3.05 us
    pallas_call x1, Pallas kernels: 118 us -> 94.6 us  [local(): pl.pallas_call(kernel, out_shape=jax.ShapeDtypeStruct(states.shape, jnp.f...]
    unnamed x3 -> x1, local copies, waits for them, and re-layouts: 5.9 us -> 3.05 us
where the time goes in v2:
time: 97.8 us; the launch traced here: 97.6 us
  Pallas kernels  94.6 us (97%)
  local copies, waits for them, and re-layouts  3.05 us (3%)
    pallas_call x1, Pallas kernels, local(): pl.pallas_call(kernel, out_shape=jax.ShapeDtypeStruct(states.shape, jnp.f...  94.6 us
    unnamed x1, local copies, waits for them, and re-layouts  3.05 us

profile of v2, /device:TPU:104, one launch (start us, length us, event | category | flops | bytes accessed | tf_op | source)
XLA Modules:
  0.0 97.6 jit_solution(9669618257072447267)
XLA Ops:
  0.0 94.6 %analysis.1 = f32[32,16384]{1,0:T(8,128)} custom-call(f32[32,16384]{1,0:T(8,128)} %states.1, f32[32,1024]{1,0:T(8,128)} %obs.1, f32[32,1024]{1,0:T(8,128)} %inn.1, s32[24,128]{1,0:T(8,128)} %bitcast.3, s32[1,128]{1,0:T(1,128)} %bitcast.5, f32[24,128]{1,0:T(8,128)} %bitcast.4), custom_call_target="tpu_custom_call" | custom-call | tf_op jit(solution)/shard_map/analysis/pallas_call | solution.py:298
  94.6 3.0 %copy.8 = f32[32,16384]{1,0:T(8,128)} copy(f32[32,16384]{1,0:T(8,128)} %analysis.1) | data formatting | bytes 4194304

commit v3 on v2

--- a/solution.py
+++ b/solution.py
@@ -17,11 +17,14 @@
 OBS = 1024
 OB = OBS // BLK
 QUART = OBS // 4
-QB = OB // 2
+INS = 2
+PART_IN = CELLS // INS
 L = 24
-SENDS = 4
+PARTS = ((0, 2), (2, 2), (4, 2), (6, 2))
+SENDS = len(PARTS)
+EARLY = (0, 0, 0)
+INS_EARLY = 1
 ORDER = (1, 4, 3, 12, 5, 15, 7, 13, 2, 8, 6, 9, 14, 11, 10)
-WIDE = CELLS // SENDS
 
 
 def split(value):
@@ -86,20 +89,20 @@
         piece = line(1, q, 0)
         return remote(piece, piece, g_send.at[q, d - 1], g_recv.at[q, d - 1], along(q, 0, d))
 
-    def second(q, d):
-        piece = plane(1, q, 0)
-        return remote(piece, piece, g_send.at[q, 2 + d], g_recv.at[q, 2 + d], along(q, 1, d))
+    def second(q, d, kind):
+        piece, n = plane(1, q, 0, kind), 2 + d + kind
+        return remote(piece, piece, g_send.at[q, n], g_recv.at[q, n], along(q, 1, d))
 
     def relay(q, d):
-        piece = plane(1, q, 4 - d, d // 2)
-        return remote(piece, piece, g_send.at[q, 6 + d // 2], g_recv.at[q, 6 + d // 2], along(q, 1, d))
+        piece, n = plane(1, q, 4 - d, d // 2), 7 + d // 2
+        return remote(piece, piece, g_send.at[q, n], g_recv.at[q, n], along(q, 1, d))
 
     def piece_of(slot, piece):
         if piece == 0:
             return wide.at[slot, :, y, x]
         if piece < 13:
             return line(slot, (piece - 1) // 3, (piece - 1) % 3 + 1)
-        return plane(slot, (piece - 13) // 3, (piece - 13) % 3 + 1)
+        return plane(slot, (piece - 13) // 6, (piece - 13) % 6 // 2 + 1, (piece - 13) % 2)
 
     def pass_on(piece, slot, n):
         return remote(
@@ -107,20 +110,22 @@
             (member, above if n == 0 else below),
         )
 
-    def cells_in(k):
+    def cells_in(k, part):
         yy, xx = lax.rem(y + k // NX, NY), lax.rem(x + k % NX, NX)
         target = yy * NX + xx
+        place = pl.multiple_of(target * CELLS + part * PART_IN, PART_IN)
         return remote(
-            states.at[:, pl.ds(pl.multiple_of(target * CELLS, CELLS), CELLS)], cols.at[member],
-            a_send.at[k - 1], a_recv.at[k - 1], (target, region),
+            states.at[:, pl.ds(place, PART_IN)], cols.at[member, :, pl.ds(part * PART_IN, PART_IN)],
+            a_send.at[part, k - 1], a_recv.at[part, k - 1], (target, region),
         )
 
     def cells_out(part, k):
         yy, xx = lax.rem(y + k // NX, NY), lax.rem(x + k % NX, NX)
         target = yy * NX + xx
-        place = pl.multiple_of(member * CELLS + part * WIDE, WIDE)
+        begin, size = (n * BLK for n in PARTS[part])
+        place = pl.multiple_of(member * CELLS + begin, BLK)
         return remote(
-            result.at[target, :, pl.ds(part * WIDE, WIDE)], out.at[:, pl.ds(place, WIDE)],
+            result.at[target, :, pl.ds(begin, size)], out.at[:, pl.ds(place, size)],
             o_send.at[part, k - 1], o_recv.at[part, k - 1], (target, region),
         )
 
@@ -133,26 +138,34 @@
             for q in pair:
                 first(q, d).wait_recv()
                 both(3 * q + 4 - d)
-        for d in (1, 3):
-            for q in pair:
-                second(q, d).start()
-
-    def planes_near(pair, onward=None):
-        for d in (1, 3):
-            for q in pair:
-                second(q, d).wait_recv()
-                relay(q, d).start()
-                if onward is None or q in onward:
-                    both(13 + 3 * q + 3 - d)
-
-    def planes_far(pair, last=()):
+        for late in (0, 1):
+            for d in (1, 3):
+                for q in pair:
+                    second(q, d, (d // 2 + late) % 2).start()
+
+    def planes_near(pair, onward):
+        for late in (0, 1):
+            for d in (1, 3):
+                for q in pair:
+                    kind = (d // 2 + late) % 2
+                    second(q, d, kind).wait_recv()
+                    if not late:
+                        relay(q, d).start()
+                    if q in onward:
+                        both(13 + 6 * q + 2 * (3 - d) + kind)
+
+    def planes_far(pair, held=()):
         for q in pair:
             for d in (1, 3):
                 relay(q, d).wait_recv()
-            both(13 + 3 * q + 1)
-            if q in last[1:]:
-                both(13 + 3 * q)
-                both(13 + 3 * q + 2)
+                both(13 + 6 * q + 2 + d // 2)
+            if q in held:
+                for piece in (0, 1, 4, 5):
+                    both(13 + 6 * q + piece)
+
+    def states_to(begin, end):
+        for n in range(begin, end):
+            cells_in(ORDER[n % (GROUP - 1)], n // (GROUP - 1)).start()
 
     own_obs.wait()
     own_inn.wait()
@@ -163,6 +176,7 @@
     both(0)
     lines((0, 1))
     lines((2, 3))
+    states_to(0, EARLY[0])
 
     start = member * CB
     ids = lists[...] - (region - 1) * OB
@@ -191,14 +205,14 @@
             lax.fori_loop(0, many, block, 0, unroll=True)
             base += many
 
-    def add(runs, new=False):
+    def add(runs, new=False, blocks=range(CB)):
         rows = [slot * OB + begin + b for slot, begin, many in runs for b in range(many)]
 
         def strip(i, carry):
             at_i = pl.ds(pl.multiple_of(i * 8, 8), 8)
             lanes = [pl.ds(k * BLK, BLK) for k in range(MEMBERS // BLK)]
             parts = [[g[b, at_i, lane] for lane in lanes] for b in range(len(rows))]
-            for c in range(CB):
+            for c in blocks:
                 sums = [None if new else w[c, at_i, lane] for lane in lanes]
                 for row, part in zip(rows, parts):
                     weight = jnp.broadcast_to(table[row, pl.ds(c, 1), :], (8, BLK))
@@ -222,25 +236,22 @@
                 target, target, f_send.at[slot // 2, piece], f_recv.at[slot // 2, piece], (member, above)
             ).wait_recv()
 
-    early = (*range(7), *range(13, 19))
-    planes_near((0, 1))
+    early = (*range(7), *range(13, 25))
+    planes_near((0, 1), (0, 1))
+    states_to(EARLY[0], EARLY[1])
     planes_far((0, 1))
     products([(1, 0, 4)])
     planes_near((2, 3), (2,))
+    states_to(EARLY[1], EARLY[2])
     add([(1, 0, 4)], True)
-    planes_far((2, 3), (2, 3))
-    for k in ORDER:
-        cells_in(k).start()
+    planes_far((2, 3), (3,))
+    states_to(EARLY[2], INS * (GROUP - 1))
     arrived(near, early)
     window((near, 0, 4))
-    arrived(near, (*range(7, 13), *range(19, 25)))
+    arrived(near, (*range(7, 13), *range(25, 37)))
     window((1, 4, 4), (near, 4, 4))
     arrived(far, early)
     window((far, 0, 4))
-
-    own_cols.wait()
-    for k in range(1, GROUP):
-        cells_in(k).wait_recv()
 
     def centre(c, carry):
         at_c = pl.ds(pl.multiple_of(c * BLK, BLK), BLK)
@@ -249,14 +260,20 @@
         cells_hl[c] = jnp.concatenate([hi, lo], axis=1)
         return carry
 
-    lax.fori_loop(0, CB, centre, 0)
-
-    arrived(far, (*range(7, 10), *range(19, 22)))
+    def cells_here(part):
+        for k in range(1, GROUP):
+            cells_in(k, part).wait_recv()
+        lax.fori_loop(part * (CB // INS), (part + 1) * (CB // INS), centre, 0)
+
+    own_cols.wait()
+    for part in range(INS_EARLY):
+        cells_here(part)
+    arrived(far, (*range(7, 10), *range(25, 31)))
     window((far, 4, 2))
-    arrived(far, (*range(10, 13), *range(22, 25)))
-    window((far, 6, 2))
-
-    for part in range(SENDS):
+    arrived(far, (*range(10, 13), *range(31, 37)))
+    products([(far, 6, 2)])
+
+    for part, (begin, many) in enumerate(PARTS):
         def finish(c, carry):
             at_c = pl.ds(pl.multiple_of(c * BLK, BLK), BLK)
             hi, lo = split(w[c])
@@ -267,7 +284,10 @@
             result[:, :, at_c] = cols[:, :, at_c] + inc.reshape(GROUP, ROWS, BLK)
             return carry
 
-        lax.fori_loop(part * (CB // SENDS), (part + 1) * (CB // SENDS), finish, 0)
+        if begin * INS % CB == 0 and begin * INS // CB >= INS_EARLY:
+            cells_here(begin * INS // CB)
+        add([(far, 6, 2)], blocks=range(begin, begin + many))
+        lax.fori_loop(begin, begin + many, finish, 0)
         for k in ORDER:
             cells_out(part, k).start()
     place = pl.multiple_of(member * CELLS, CELLS)
@@ -278,13 +298,15 @@
         for d in (1, 2, 3):
             first(q, d).wait_send()
         for d in (1, 3):
-            second(q, d).wait_send()
+            second(q, d, 0).wait_send()
+            second(q, d, 1).wait_send()
             relay(q, d).wait_send()
-    for piece in range(25):
+    for piece in range(37):
         pass_on(piece, 0, 0).wait_send()
         pass_on(piece, 2, 1).wait_send()
-    for k in range(1, GROUP):
-        cells_in(k).wait_send()
+    for part in range(INS):
+        for k in range(1, GROUP):
+            cells_in(k, part).wait_send()
     for part in range(SENDS):
         for k in range(1, GROUP):
             cells_out(part, k).wait()
@@ -297,9 +319,9 @@
     dma = pltpu.SemaphoreType.DMA
     return pl.pallas_call(
         kernel,
-        out_shape=jax.ShapeDtypeStruct(states.shape, jnp.float32),
+        out_shape=pltpu.VMEM(states.shape, jnp.float32),
         in_specs=[hbm, hbm, hbm, vmem, vmem, vmem],
-        out_specs=hbm,
+        out_specs=vmem,
         scratch_shapes=[
             pltpu.VMEM((3, 2, NY, NX, ROWS, OBS), jnp.float32),
             pltpu.VMEM((GROUP, ROWS, CELLS), jnp.float32),
@@ -309,17 +331,17 @@
             pltpu.VMEM((3 * OB, CB, BLK), jnp.float32),
             pltpu.VMEM((GROUP, ROWS, CELLS), jnp.float32),
             dma((4,)),
-            dma((4, 8)),
-            dma((4, 8)),
-            dma((2, 25)),
-            dma((2, 25)),
-            dma((GROUP - 1,)),
-            dma((GROUP - 1,)),
+            dma((4, 9)),
+            dma((4, 9)),
+            dma((2, 37)),
+            dma((2, 37)),
+            dma((INS, GROUP - 1)),
+            dma((INS, GROUP - 1)),
             dma((SENDS, GROUP - 1)),
             dma((SENDS, GROUP - 1)),
         ],
         compiler_params=pltpu.CompilerParams(
-            collective_id=0, has_side_effects=True, vmem_limit_bytes=56 * 2**20
+            collective_id=0, has_side_effects=True, vmem_limit_bytes=58 * 2**20
         ),
         name="analysis",
     )(states, obs_ens, innovation, lists.T, counts.reshape(1, -1), taper.T)

time: 97.8 us -> 89.7 us (0.917)
  the two profiles are of different devices: /device:TPU:104 before, /device:TPU:1 now
where the time goes in v3:
time: 89.7 us; the launch traced here: 89.6 us
  Pallas kernels  88.3 us (98%)
  local copies, waits for them, and re-layouts  1.32 us (1%)
    pallas_call x1, Pallas kernels, local(): pl.pallas_call(kernel, out_shape=pltpu.VMEM(states.shape, jnp.float32), i...  88.3 us

profile of v3, /device:TPU:1, one launch (start us, length us, event | category | flops | bytes accessed | tf_op | source)
XLA Modules:
  0.0 89.6 jit_solution(12628569931616332919)
XLA Ops:
  0.0 88.3 %analysis.1 = f32[32,16384]{1,0:T(8,128)S(1)} custom-call(f32[32,16384]{1,0:T(8,128)} %states.1, f32[32,1024]{1,0:T(8,128)} %obs.1, f32[32,1024]{1,0:T(8,128)} %inn.1, s32[24,128]{1,0:T(8,128)} %bitcast.3, s32[1,128]{1,0:T(1,128)} %bitcast.5, f32[24,128]{1,0:T(8,128)} %bitcast.4), custom_call_target="tpu_custom_call" | custom-call | tf_op jit(solution)/shard_map/analysis/pallas_call | solution.py:320
  88.3 1.3 %copy.8 = f32[32,16384]{1,0:T(8,128)} copy(f32[32,16384]{1,0:T(8,128)S(1)} %analysis.1) | data formatting | bytes 4194304

commit v4 on v3

--- a/solution.py
+++ b/solution.py
@@ -20,7 +20,7 @@
 INS = 2
 PART_IN = CELLS // INS
 L = 24
-PARTS = ((0, 2), (2, 2), (4, 2), (6, 2))
+PARTS = ((0, 1), (1, 1), (2, 2), (4, 2), (6, 2))
 SENDS = len(PARTS)
 EARLY = (0, 0, 0)
 INS_EARLY = 1
@@ -129,9 +129,14 @@
             o_send.at[part, k - 1], o_recv.at[part, k - 1], (target, region),
         )
 
+    far_region = lax.rem(region + regions - 1 + 2 * core, regions)
+    near_region = region + 1 - 2 * core
+
     def both(piece):
-        pass_on(piece, 0, 0).start()
-        pass_on(piece, 2, 1).start()
+        for n, slot, device in ((1 - core, 2 - 2 * core, far_region), (core, 2 * core, near_region)):
+            remote(
+                piece_of(1, piece), piece_of(slot, piece), f_send.at[n, piece], f_recv.at[n, piece], (member, device)
+            ).start()
 
     def lines(pair):
         for d in (1, 3, 2):

time: 89.7 us -> 89.1 us (level)
  the two profiles are of different devices: /device:TPU:1 before, /device:TPU:4 now
where the time goes in v4:
time: 89.1 us; the launch traced here: 89 us
  Pallas kernels  87.6 us (98%)
  local copies, waits for them, and re-layouts  1.32 us (1%)
    pallas_call x1, Pallas kernels, local(): pl.pallas_call(kernel, out_shape=pltpu.VMEM(states.shape, jnp.float32), i...  87.6 us

profile of v4, /device:TPU:4, one launch (start us, length us, event | category | flops | bytes accessed | tf_op | source)
XLA Modules:
  0.0 89.0 jit_solution(18221655561012132187)
XLA Ops:
  0.0 87.6 %analysis.1 = f32[32,16384]{1,0:T(8,128)S(1)} custom-call(f32[32,16384]{1,0:T(8,128)} %states.1, f32[32,1024]{1,0:T(8,128)} %obs.1, f32[32,1024]{1,0:T(8,128)} %inn.1, s32[24,128]{1,0:T(8,128)} %bitcast.3, s32[1,128]{1,0:T(1,128)} %bitcast.5, f32[24,128]{1,0:T(8,128)} %bitcast.4), custom_call_target="tpu_custom_call" | custom-call | tf_op jit(solution)/shard_map/analysis/pallas_call | solution.py:325
  87.6 1.3 %copy.8 = f32[32,16384]{1,0:T(8,128)} copy(f32[32,16384]{1,0:T(8,128)S(1)} %analysis.1) | data formatting | bytes 4194304

commit v5 on v3

--- a/solution.py
+++ b/solution.py
@@ -20,10 +20,11 @@
 INS = 2
 PART_IN = CELLS // INS
 L = 24
-PARTS = ((0, 2), (2, 2), (4, 2), (6, 2))
+PARTS = ((0, 1), (1, 1), (2, 2), (4, 2), (6, 2))
 SENDS = len(PARTS)
-EARLY = (0, 0, 0)
+EARLY = (0, 0, 8)
 INS_EARLY = 1
+CROSSED = tuple(13 + 6 * q + 2 * (3 - d) + d // 2 for q in (2, 3) for d in (1, 3))
 ORDER = (1, 4, 3, 12, 5, 15, 7, 13, 2, 8, 6, 9, 14, 11, 10)
 
 
@@ -35,7 +36,7 @@
 def kernel(
     states, obs, inn, lists, counts, taper, out,
     wide, cols, cells_hl, g, w, table, result,
-    local_sem, g_send, g_recv, f_send, f_recv, a_send, a_recv, o_send, o_recv,
+    local_sem, g_send, g_recv, f_send, f_recv, x_send, x_recv, a_send, a_recv, o_send, o_recv,
 ):
     member = lax.axis_index("member")
     region = lax.axis_index("region")
@@ -104,11 +105,24 @@
             return line(slot, (piece - 1) // 3, (piece - 1) % 3 + 1)
         return plane(slot, (piece - 13) // 6, (piece - 13) % 6 // 2 + 1, (piece - 13) % 2)
 
-    def pass_on(piece, slot, n):
+    far_region = lax.rem(region + regions - 1 + 2 * core, regions)
+    near_region = region + 1 - 2 * core
+
+    def to_far(piece):
+        n, slot = 1 - core, 2 - 2 * core
         return remote(
-            piece_of(1, piece), piece_of(slot, piece), f_send.at[n, piece], f_recv.at[n, piece],
-            (member, above if n == 0 else below),
-        )
+            piece_of(1, piece), piece_of(slot, piece), f_send.at[n, piece], f_recv.at[n, piece], (member, far_region)
+        )
+
+    def to_near(piece):
+        n, slot = core, 2 * core
+        return remote(
+            piece_of(1, piece), piece_of(slot, piece), f_send.at[n, piece], f_recv.at[n, piece], (member, near_region)
+        )
+
+    def across(q, d):
+        piece, n = plane(2 * core, q, 0, d // 2), (q - 2) * 2 + d // 2
+        return remote(piece, piece, x_send.at[n], x_recv.at[n], along(q, 1, d))
 
     def cells_in(k, part):
         yy, xx = lax.rem(y + k // NX, NY), lax.rem(x + k % NX, NX)
@@ -130,8 +144,9 @@
         )
 
     def both(piece):
-        pass_on(piece, 0, 0).start()
-        pass_on(piece, 2, 1).start()
+        if piece not in CROSSED:
+            to_far(piece).start()
+        to_near(piece).start()
 
     def lines(pair):
         for d in (1, 3, 2):
@@ -221,7 +236,7 @@
                     w[c, at_i, lane] = total
             return carry
 
-        lax.fori_loop(0, MEMBERS // 8, strip, 0, unroll=2)
+        lax.fori_loop(0, MEMBERS // 8, strip, 0, unroll=4)
 
     def window(*runs):
         products(runs)
@@ -245,12 +260,16 @@
     states_to(EARLY[1], EARLY[2])
     add([(1, 0, 4)], True)
     planes_far((2, 3), (3,))
+    arrived(far, (0, *range(7, 13)))
+    for q in (2, 3):
+        for d in (1, 3):
+            across(q, d).start()
     states_to(EARLY[2], INS * (GROUP - 1))
     arrived(near, early)
     window((near, 0, 4))
     arrived(near, (*range(7, 13), *range(25, 37)))
     window((1, 4, 4), (near, 4, 4))
-    arrived(far, early)
+    arrived(far, early[1:])
     window((far, 0, 4))
 
     def centre(c, carry):
@@ -268,9 +287,13 @@
     own_cols.wait()
     for part in range(INS_EARLY):
         cells_here(part)
-    arrived(far, (*range(7, 10), *range(25, 31)))
+    arrived(far, [piece for piece in range(25, 31) if piece not in CROSSED])
+    for d in (1, 3):
+        across(2, d).wait_recv()
     window((far, 4, 2))
-    arrived(far, (*range(10, 13), *range(31, 37)))
+    arrived(far, [piece for piece in range(31, 37) if piece not in CROSSED])
+    for d in (1, 3):
+        across(3, d).wait_recv()
     products([(far, 6, 2)])
 
     for part, (begin, many) in enumerate(PARTS):
@@ -302,8 +325,12 @@
             second(q, d, 1).wait_send()
             relay(q, d).wait_send()
     for piece in range(37):
-        pass_on(piece, 0, 0).wait_send()
-        pass_on(piece, 2, 1).wait_send()
+        if piece not in CROSSED:
+            to_far(piece).wait_send()
+        to_near(piece).wait_send()
+    for q in (2, 3):
+        for d in (1, 3):
+            across(q, d).wait_send()
     for part in range(INS):
         for k in range(1, GROUP):
             cells_in(k, part).wait_send()
@@ -335,6 +362,8 @@
             dma((4, 9)),
             dma((2, 37)),
             dma((2, 37)),
+            dma((4,)),
+            dma((4,)),
             dma((INS, GROUP - 1)),
             dma((INS, GROUP - 1)),
             dma((SENDS, GROUP - 1)),

time: 89.7 us -> 88.6 us (0.988)
  the two profiles are of different devices: /device:TPU:1 before, /device:TPU:104 now
where the time goes in v5:
time: 88.6 us; the launch traced here: 88.1 us
  Pallas kernels  86.7 us (98%)
  local copies, waits for them, and re-layouts  1.32 us (1%)
    pallas_call x1, Pallas kernels, local(): pl.pallas_call(kernel, out_shape=pltpu.VMEM(states.shape, jnp.float32), i...  86.7 us

profile of v5, /device:TPU:104, one launch (start us, length us, event | category | flops | bytes accessed | tf_op | source)
XLA Modules:
  0.0 88.1 jit_solution(7344276108203352489)
XLA Ops:
  0.0 86.7 %analysis.1 = f32[32,16384]{1,0:T(8,128)S(1)} custom-call(f32[32,16384]{1,0:T(8,128)} %states.1, f32[32,1024]{1,0:T(8,128)} %obs.1, f32[32,1024]{1,0:T(8,128)} %inn.1, s32[24,128]{1,0:T(8,128)} %bitcast.3, s32[1,128]{1,0:T(1,128)} %bitcast.5, f32[24,128]{1,0:T(8,128)} %bitcast.4), custom_call_target="tpu_custom_call" | custom-call | tf_op jit(solution)/shard_map/analysis/pallas_call | solution.py:347
  86.7 1.3 %copy.8 = f32[32,16384]{1,0:T(8,128)} copy(f32[32,16384]{1,0:T(8,128)S(1)} %analysis.1) | data formatting | bytes 4194304
